TPU v7x, 32 devices: a whole 2x2x4 slice. The times are simulated.
32 devices in a mesh: atm: 8 (over z, y), cpl: 4 (over x, core).
Axes of the slice: x: 2, y: 2, z: 4, core: 2. Of those that a mesh axis runs over, the one named last changes fastest.
Arguments:
- air_temp: float32 [192, 64, 512], P('atm', None, 'cpl'), may hold values from -6 to 6
- wind_field: bfloat16 [2, 192, 64, 512], P(None, 'atm', None, 'cpl'), may hold values from -0.3984375 to 0.3984375
- physics: float32 [64, 64], replicated, may hold values from -0.75 to 0.75
- sea_surface: float32 [192, 512], P('atm', 'cpl'), may hold values from -6 to 6
- shortwave: float32 [192, 512], P('atm', 'cpl'), may hold values from 0 to 1
- ocean_mask: int32 [192, 512], P('atm', 'cpl'), may hold values 0 or 1
- owner_route: int32 [4, 192, 1], P('cpl', 'atm'), may hold values from 0 to 3; in each aligned block of 24 rows (0 to 23, 24 to 47, ..., all dimensions but the last counted through in order) at most 12 rows name the same one
- ocean_tile: int32 [4, 192], P('cpl', 'atm'), may hold values from 0 to 23
- weight_tile: int32 [4, 192], P('cpl', 'atm'), may hold values from 0 to 15
- remap_tiles: float32 [16, 32, 128], replicated, may hold values from 0.002 to 0.03
- ocean_temp: float32 [80, 24576], P(None, ('atm', 'cpl')), may hold values from -6 to 6
- mixing: float32 [80, 80], replicated, may hold values from -0.625 to 0.625
Outputs:
- air_next: float32 [192, 64, 512], P('atm', None, 'cpl')
- ocean_next: float32 [80, 24576], P(None, ('atm', 'cpl'))
- surface_temp: float32 [192, 512], P('atm', 'cpl')
Inputs may be any that keep to these rules, and one draw needn't show every extreme that they name: `owner_route`: among the 24 tiles of one device at most 12 name the same owner, and in every draw some device's tiles name one owner exactly 12 times. `ocean_tile`: ocean tile index within the owner. `weight_tile`: row of remap_tiles used by the tile.
All inputs are finite; a program needn't handle non-finite values. No bound on the sum of `ocean_mask` on one device may be relied on, other than what follows from the above.
Results may differ from a plain program's by a relative error of at most 0.0015.
Values may be sent and summed in bfloat16 or wider, within the bound.
No kernel may reach another device: no remote copies, remote signals or barrier semaphores. Data moves between devices by JAX's collectives and lax.ppermute only.
A program may use at most 64 MiB of HBM per device.

v0:
```python
import jax
import jax.numpy as jnp
from jax import lax
from jax.experimental import pallas as pl
from jax.experimental.pallas import tpu as pltpu
from jax.sharding import PartitionSpec as P

diffusion_rate = 0.05
physics_rate = 0.5
highest = lax.Precision.HIGHEST
f32 = jnp.float32
bf16 = jnp.bfloat16


def pair_even(count):
    return [(i, i ^ 1) for i in range(count)]


def pair_odd(count):
    up = [(i, (i + 1) % count) for i in range(1, count, 2)]
    return up + [(target, source) for source, target in up]


def exchange(to_even, to_odd, axis):
    count = lax.axis_size(axis)
    odd_side = lax.ppermute(to_odd, axis, pair_odd(count))
    even_side = lax.ppermute(to_even, axis, pair_even(count))
    return even_side, odd_side


def shift(block, axis, turn):
    count = lax.axis_size(axis)
    return lax.ppermute(block, axis, [(i, (i + turn) % count) for i in range(count)])


def iota(shape, dim):
    return lax.broadcasted_iota(jnp.int32, shape, dim)


def roll(value, shift):
    return pltpu.roll(value, shift % value.shape[-1], value.ndim - 1)


def pick(flag, yes, no):
    return jnp.where(flag, yes, no)


def rates(first, second):
    return (
        jnp.maximum(first, 0.0) + diffusion_rate,
        diffusion_rate - jnp.minimum(first, 0.0),
        jnp.maximum(second, 0.0) + diffusion_rate,
        diffusion_rate - jnp.minimum(second, 0.0),
    )


def split(value):
    high = value.astype(bf16)
    return high, (value - high.astype(f32)).astype(bf16)


def physics_stack(physics):
    high, low = split(physics)
    return jnp.concatenate([high, high, low], axis=1)


def column(stack, field):
    high, low = split(field)
    tendency = jnp.dot(
        stack, jnp.concatenate([high, low, high], axis=0), preferred_element_type=f32
    )
    return field + physics_rate * jnp.tanh(tendency)


def pack_kernel(
    air, wind, physics, mixing,
    packed, to_even, to_odd, air_here, wind_here, physics_here, mixing_here, sems, square_sems,
):
    rows, levels, width = air.shape
    lane = iota((levels, width), 1)
    place = lane // 4
    kind = lane % 4
    squares = [
        pltpu.make_async_copy(physics, physics_here, square_sems.at[0]),
        pltpu.make_async_copy(mixing, mixing_here, square_sems.at[1]),
    ]
    for copy in squares:
        copy.start()
    parts = sems.shape[1]
    size = rows // parts
    copies = []
    for part in range(parts):
        span = pl.ds(part * size, size)
        copies.append(
            (
                pltpu.make_async_copy(air.at[span], air_here.at[span], sems.at[0, part]),
                pltpu.make_async_copy(wind.at[:, span], wind_here.at[:, span], sems.at[1, part]),
            )
        )
        for copy in copies[-1]:
            copy.start()
    cells = jnp.zeros((levels, width), bf16)
    first = jnp.zeros((levels, width), bf16)
    second = jnp.zeros((levels, width), bf16)
    for x in range(rows):
        if x % size == 0:
            for copy in copies[x // size]:
                copy.wait()
        here = place == x
        cells = pick(here, roll(air_here[x].astype(bf16), 4 * x + 2), cells)
        first = pick(here, roll(wind_here[0, x], 4 * x + 2), first)
        second = pick(here, roll(wind_here[1, x], 4 * x + 2), second)
    to_high = pick(kind < 2, cells, pick(kind == 2, roll(first, 1), roll(second, 2)))
    to_low = pick(kind >= 2, cells, pick(kind == 0, roll(first, -2), roll(second, -1)))
    upper = lax.axis_index("cpl") % 2 == 0
    packed[...] = cells.astype(f32)
    to_even[...] = pick(upper, to_high, to_low)
    to_odd[...] = pick(upper, to_low, to_high)
    for copy in squares:
        copy.wait()


def cpl_sides(even_side, odd_side):
    upper = lax.axis_index("cpl") % 2 == 0
    high = pick(upper, even_side[...].astype(f32), odd_side[...].astype(f32))
    low = pick(upper, odd_side[...].astype(f32), even_side[...].astype(f32))
    return low, high


def outer_cells(low, high):
    kind = iota(low.shape, 1) % 4
    return pick(kind < 2, low, high)


def swap_cells(cells):
    kind = iota(cells.shape, 1) % 4
    return pick(kind == 2, roll(cells, 1), roll(cells, -1))


def sideways(field, swapped, x):
    width = field.shape[1]
    lane = iota(field.shape, 1)
    halo = roll(swapped, -(4 * x + 2))
    south = pick(lane == 0, halo, roll(field, 1))
    north = pick(lane == width - 1, halo, roll(field, -1))
    return south, north


def sideways_of(field, cells, x):
    width = field.shape[1]
    lane = iota(field.shape, 1)
    south = pick(lane == 0, roll(cells, -(4 * x + 1)), roll(field, 1))
    north = pick(lane == width - 1, roll(cells, -(4 * x + 3)), roll(field, -1))
    return south, north


def advance_row(center, west, east, south, north, first, second):
    around = (west + east) + (south + north)
    upwind_first = jnp.where(first > 0.0, west, east) - center
    upwind_second = jnp.where(second > 0.0, south, north) - center
    return ((1.0 - 4.0 * diffusion_rate) * center + diffusion_rate * around) + (
        jnp.abs(first) * upwind_first + jnp.abs(second) * upwind_second
    )


def advance_outer(own, low, high, outer, west, east):
    kind = iota(outer.shape, 1) % 4
    south = roll(pick(kind == 0, outer, own), 1)
    north = roll(pick(kind == 3, outer, own), -1)
    first = pick(kind == 1, roll(low, -1), roll(high, 2))
    second = pick(kind == 1, roll(low, -2), roll(high, 1))
    return advance_row(outer, west, east, south, north, first, second)


def pack_corners(outer, x):
    levels, width = outer.shape
    place = iota((8, width), 1) // 4
    held = jnp.zeros((8, width), f32)
    for at in range(levels // 8):
        held = pick(place == at, roll(outer[8 * at : 8 * at + 8], 4 * (at - x)), held)
    return jnp.concatenate([held, jnp.zeros_like(held)], axis=0)


def unpack_corners(held, levels, x):
    return jnp.concatenate([roll(held[0:8], 4 * (x - at)) for at in range(levels // 8)], axis=0)


def make_edge_kernel(rows, upper):
    def edge_kernel(air, wind, even_side, odd_side, _, message, partial):
        low, high = cpl_sides(even_side, odd_side)
        outer = outer_cells(low, high)
        at, beside = (rows - 1, rows - 2) if upper else (0, 1)
        center, inner = air[at], air[beside]
        levels = center.shape[0]
        cw, ce, cs, cn = rates(wind[0, at].astype(f32), wind[1, at].astype(f32))
        inside, outside = (cw, ce) if upper else (ce, cw)
        south, north = sideways_of(center, outer, rows - 1 if upper else 0)
        known = (
            center
            + (inside * (inner - center) - outside * center)
            + (cs * (south - center) + cn * (north - center))
        )
        partial[0] = known
        partial[1] = outside
        for part, value in enumerate((center, known, outside)):
            message[part * levels : (part + 1) * levels] = value.astype(bf16)
        message[3 * levels :] = pack_corners(outer, rows - 1 if upper else 0).astype(bf16)

    return edge_kernel


def inner_kernel(
    air, wind, stack_ref, own, even_side, odd_side, ready, near, bottom, field
):
    rows, levels, width = air.shape
    low, high = cpl_sides(even_side, odd_side)
    outer = outer_cells(low, high)
    stack = stack_ref[...]
    swapped = swap_cells(outer)
    after = advance_outer(
        own[...], low, high, outer, roll(outer, 4), roll(outer, -4)
    )
    swapped_after = swap_cells(column(stack, after))

    def step(source, halo, x):
        center = source[x]
        south, north = sideways(center, halo, x)
        first, second = wind[0, x].astype(f32), wind[1, x].astype(f32)
        return advance_row(center, source[x - 1], source[x + 1], south, north, first, second)

    def pair(source, halo, x):
        return column(stack, jnp.concatenate([step(source, halo, x), step(source, halo, x + 1)], axis=1))

    for x in range(1, rows - 1, 2):
        both = pair(air, swapped, x)
        field[x] = both[:, :width]
        field[x + 1] = both[:, width:]
    near[0] = field[1]
    near[1] = field[2]
    near[2] = field[rows - 3]
    near[3] = field[rows - 2]
    bottom[...] = jnp.zeros_like(bottom)
    for x in range(2, rows - 2, 2):
        both = pair(field, swapped_after, x)
        ready[x] = both[:, :width]
        ready[x + 1] = both[:, width:]
        bottom[x : x + 1] = both[0:1, :width]
        bottom[x + 1 : x + 2] = both[0:1, width:]


def as_column(row):
    size = row.shape[1]
    square = jnp.broadcast_to(row, (size, size))
    return jnp.sum(
        jnp.where(iota((size, size), 0) == iota((size, size), 1), square, 0.0),
        axis=1,
        keepdims=True,
    )


def fold(value, size):
    span = value.shape[1] // 2
    while span >= size:
        value = value + roll(value, span)
        span //= 2
    return value


def chosen_shares(fluxes, halves, bank, ocean_width):
    rows, width = fluxes[0].shape
    high, low = split(jnp.concatenate(fluxes, axis=0))
    every = jnp.dot(
        jnp.concatenate([high, low, high], axis=1), halves, preferred_element_type=f32
    )
    shares = []
    for part in range(len(fluxes)):
        total = jnp.zeros((rows, width), f32)
        for at in range(0, halves.shape[1], width):
            block = (iota((rows, width), 1) + at) // ocean_width
            mine = every[part * rows : (part + 1) * rows, at : at + width]
            total = total + jnp.where(block == bank, mine, 0.0)
        shares.append(fold(total, ocean_width))
    return shares


def start_kernel(winds, physics, mixing, _, *refs):
    count = 8
    far = refs[:count]
    mask, sea, weights, ocean, exchange_rate, sun, bank_near, message, wanted, forward, stack = refs[
        count : count + 11
    ]
    route, tile, shortwave, bank, sems = refs[count + 11 :]
    here = (route, tile, shortwave, bank, mask, sea, weights, ocean)
    copies = [
        pltpu.make_async_copy(source, target, sems.at[at])
        for at, (source, target) in enumerate(zip(far, here))
    ]
    for copy in copies:
        copy.start()
    rows, width = shortwave.shape
    banks, ocean_width, _ = weights.shape
    depth = ocean.shape[0]
    lane = iota((rows, width), 1)
    group = lax.axis_index("cpl")
    for x in range(rows):
        first = winds[0, x, 0:16].astype(f32)[0:1]
        second = winds[1, x, 0:16].astype(f32)[0:1]
        exchange_rate[x : x + 1] = first * first + second * second
    level = iota((depth, width), 0)
    profile = jnp.exp(level.astype(f32) / -8.0)
    profile = profile / jnp.sum(profile, axis=0, keepdims=True)
    unit = jnp.where(iota((depth, width), 1) == 0, (level == 0).astype(f32), profile)
    message[...] = jnp.full(message.shape, -1.0, f32)
    for copy in copies:
        copy.wait()
    stack[...] = physics_stack(physics[...])
    frac = mask[...].astype(f32)
    exchange_rate[...] = frac * (0.5 + 2.0 * jnp.sqrt(exchange_rate[...] + 0.01))
    target = route[...] * rows + tile[...]
    target_at = as_column(target.astype(f32))
    own_at = (group * rows + iota((rows, 1), 0)).astype(f32)
    wanted[0:rows] = jnp.broadcast_to(target_at, (rows, width))
    wanted[rows : 2 * rows] = jnp.broadcast_to(own_at, (rows, width))
    for at in (0, 2 * ocean_width):
        message[rows : rows + 1, at : at + rows] = target.astype(f32)
        message[rows : rows + 1, at + ocean_width : at + ocean_width + rows] = (
            group * rows + iota((1, rows), 1)
        ).astype(f32)
    bank_at = as_column(bank[...].astype(f32)).astype(jnp.int32)
    high, low = split(weights[...].reshape(banks * ocean_width, width).T)
    forward[...] = jnp.concatenate([high, high, low], axis=0)
    sun[...] = frac * shortwave[...]
    bank_near[...] = jnp.broadcast_to(bank_at, (rows, width))
    top = mixing[0:8]
    settled = 0.5 * ocean[0:8] + jnp.dot(
        top, ocean[...], precision=highest, preferred_element_type=f32
    )
    answer = 0.5 * unit[0:8] + jnp.dot(top, unit, precision=highest, preferred_element_type=f32)
    surface = jnp.zeros((rows, width), f32)
    for at in range(0, rows * ocean_width, width):
        spread = jnp.broadcast_to(settled[0:1, at : at + width], (rows, width))
        surface = surface + jnp.where((lane + at) // ocean_width == iota((rows, width), 0), spread, 0.0)
    surface = fold(surface, ocean_width)
    message[0:rows, :] = surface
    message[rows + 1 : rows + 2, :] = jnp.broadcast_to(answer[0:1, 0:1], (1, width))
    message[rows + 2 : rows + 3, :] = jnp.broadcast_to(answer[0:1, 1:2], (1, width))


def make_outer_kernel(rows):
    def outer_kernel(
        above_ref, below_ref, partial_low, partial_high, air, wind, own, even_side, odd_side,
        near, stack_ref, bottom, rate, sun, sea, bank, forward, start,
        air_edges, bottom_next, message,
    ):
        width = sea.shape[1]
        ocean_width = start.shape[0]
        levels = air.shape[1]
        above = [above_ref[at * levels : (at + 1) * levels].astype(f32) for at in range(3)]
        below = [below_ref[at * levels : (at + 1) * levels].astype(f32) for at in range(3)]
        above.append(unpack_corners(above_ref[3 * levels :].astype(f32), levels, rows - 1))
        below.append(unpack_corners(below_ref[3 * levels :].astype(f32), levels, 0))
        low, high = cpl_sides(even_side, odd_side)
        outer = outer_cells(low, high)
        stack = stack_ref[...]
        place = iota(outer.shape, 1) // 4
        after = advance_outer(
            own[...],
            low,
            high,
            outer,
            pick(place == 0, below[3], roll(outer, 4)),
            pick(place == rows - 1, above[3], roll(outer, -4)),
        )
        moved = jnp.concatenate(
            [
                below[1] + below[2] * air[0],
                partial_low[0] + partial_low[1] * below[0],
                partial_high[0] + partial_high[1] * above[0],
                above[1] + above[2] * air[rows - 1],
                after,
            ],
            axis=1,
        )
        stepped = column(stack, moved)
        parts = [stepped[:, at * width : (at + 1) * width] for at in range(5)]
        inner = [near[at] for at in range(4)]
        bottom_next[...] = bottom[...]
        cells = []
        for center, west, east, x in (
            (parts[1], parts[0], inner[0], 0),
            (inner[0], parts[1], inner[1], 1),
            (inner[3], inner[2], parts[2], rows - 2),
            (parts[2], inner[3], parts[3], rows - 1),
        ):
            south, north = sideways_of(center, parts[4], x)
            first, second = wind[0, x].astype(f32), wind[1, x].astype(f32)
            cells.append(advance_row(center, west, east, south, north, first, second))
        final = column(stack, jnp.concatenate(cells, axis=1))
        for at, x in enumerate((0, 1, rows - 2, rows - 1)):
            row = final[:, at * width : (at + 1) * width]
            air_edges[at] = row
            bottom_next[x : x + 1] = row[0:1]
        heat = rate[...] * (bottom_next[...] - sea[...])
        shares, solar = chosen_shares(
            [heat, sun[...]], forward[...], bank[...], ocean_width
        )
        message[...] = start[...]
        block = iota((rows, width), 1) // ocean_width
        raised = start[rows + 1 : rows + 2, :] * shares + start[rows + 2 : rows + 3, :] * solar
        message[0:rows, :] = jnp.where(
            block == 0,
            shares,
            jnp.where(block == 1, solar, jnp.where(block == 2, raised, start[0:rows, :])),
        )

    return outer_kernel


def settle_kernel(
    edges, inner, bank, weights, ocean, mixing, out, base, response, total_weight, backward, sems
):
    rows = out.shape[0]
    middle = pl.ds(2, rows - 4)
    copies = [
        pltpu.make_async_copy(inner.at[middle], out.at[middle], sems.at[2]),
        pltpu.make_async_copy(edges.at[pl.ds(0, 2)], out.at[pl.ds(0, 2)], sems.at[0]),
        pltpu.make_async_copy(edges.at[pl.ds(2, 2)], out.at[pl.ds(rows - 2, 2)], sems.at[1]),
    ]
    for copy in copies:
        copy.start()
    width = total_weight.shape[1]
    depth = ocean.shape[0]
    banks, ocean_width, _ = weights.shape
    high, low = split(weights[...].reshape(banks * ocean_width, width))
    backward[...] = jnp.concatenate([high, high, low], axis=0)
    sums = jnp.concatenate(
        [jnp.sum(weights[at], axis=0, keepdims=True) for at in range(banks)], axis=0
    )
    hot = (iota((rows, banks), 1) == bank[:, 0:banks]).astype(f32)
    total_weight[...] = jnp.dot(hot, sums, precision=highest, preferred_element_type=f32)
    mixed = mixing[...]
    held = ocean[...]
    base[...] = 0.5 * held + jnp.dot(mixed, held, precision=highest, preferred_element_type=f32)
    level = iota((depth, width), 0)
    profile = jnp.exp(level.astype(f32) / -8.0)
    profile = profile / jnp.sum(profile, axis=0, keepdims=True)
    part = iota((depth, width), 1)
    unit = jnp.where(part == 0, (level == 0).astype(f32), jnp.where(part == 1, profile, 0.0))
    response[...] = 0.5 * unit + jnp.dot(mixed, unit, precision=highest, preferred_element_type=f32)
    for copy in copies:
        copy.wait()


def make_last_kernel(count):
    def last_kernel(*refs):
        messages, (wanted, base, response, total_weight, bottom, mask, bank, backward, ocean_next, surface, ocean_here, surface_here, sems) = (
            refs[:count],
            refs[count:],
        )
        own = messages[0][...]
        if len(messages) == 2 and len(messages[1].shape) == 3:
            blocks = [messages[1][at] for at in range(messages[1].shape[0])]
        else:
            blocks = [ref[...] for ref in messages]
        rows, width = bottom.shape
        slots = own.shape[0]
        ocean_width = slots
        cells = backward.shape[0] // 3
        lane = iota((slots, width), 1)
        labels = []
        values = []
        for block in blocks:
            labels.append(block[rows : rows + 1, :])
            values.append(jnp.where(lane < 3 * ocean_width, block, 0.0))
            values.append(jnp.where(lane < 3 * ocean_width, 0.0, block))
        left = iota((1, width), 1) < 2 * ocean_width
        hot = [
            (wanted[...] == jnp.where(left, labels[at], labels[at + 1])).astype(f32).astype(bf16)
            for at in range(0, len(labels), 2)
        ]
        high, low = split(jnp.concatenate(values, axis=0))
        got = jnp.dot(
            jnp.concatenate(hot + hot, axis=1),
            jnp.concatenate([high, low], axis=0),
            preferred_element_type=f32,
        )
        near = iota((rows, width), 1)
        seen = fold(jnp.where(near >= 2 * ocean_width, got[0:rows], 0.0), ocean_width)
        bank_at = bank[...]
        high, low = split(
            jnp.concatenate(
                [
                    jnp.where((near + at) // ocean_width == bank_at, seen, 0.0)
                    for at in range(0, cells, width)
                ],
                axis=1,
            )
        )
        weighted = jnp.dot(
            jnp.concatenate([high, low, high], axis=1), backward[...], preferred_element_type=f32
        )
        forcing = got[rows : 2 * rows]
        heat = fold(jnp.where(near < ocean_width, forcing, 0.0), ocean_width)
        solar = fold(
            jnp.where((near >= ocean_width) & (near < 2 * ocean_width), forcing, 0.0), ocean_width
        )
        first = response[:, 0:1]
        second = response[:, 1:2]
        for at in range(0, base.shape[1], width):
            mine = (near + at) // ocean_width == iota((rows, width), 0)
            heat_row = jnp.sum(jnp.where(mine, heat, 0.0), axis=0, keepdims=True)
            solar_row = jnp.sum(jnp.where(mine, solar, 0.0), axis=0, keepdims=True)
            ocean_here[:, at : at + width] = base[:, at : at + width] + (
                first * heat_row + second * solar_row
            )
        ocean_out = pltpu.make_async_copy(ocean_here, ocean_next, sems.at[0])
        ocean_out.start()
        frac = mask[...].astype(f32)
        surface_here[...] = frac * (weighted / total_weight[...]) + (1.0 - frac) * bottom[...]
        surface_out = pltpu.make_async_copy(surface_here, surface, sems.at[1])
        surface_out.start()
        ocean_out.wait()
        surface_out.wait()

    return last_kernel


def shape_of(shape, dtype=f32):
    return jax.ShapeDtypeStruct(shape, dtype)


def whole(count):
    return [pl.BlockSpec(memory_space=pltpu.VMEM) for _ in range(count)]


def in_hbm(value):
    return pltpu.with_memory_space_constraint(value, pltpu.HBM)


params = pltpu.CompilerParams(vmem_limit_bytes=48 * 1024 * 1024)


def local(
    air_temp,
    wind_field,
    physics,
    sea_surface,
    shortwave,
    ocean_mask,
    owner_route,
    ocean_tile,
    weight_tile,
    remap_tiles,
    ocean_temp,
    mixing,
):
    rows, levels, width = air_temp.shape
    groups = lax.axis_size("cpl")
    ocean_width = remap_tiles.shape[1]
    slots = ocean_width
    ocean_shape = ocean_temp.shape

    packed, to_even, to_odd, air_here, wind_here, physics, mixing = pl.pallas_call(
        pack_kernel,
        out_shape=(
            pltpu.VMEM((levels, width), f32),
            pltpu.VMEM((levels, width), bf16),
            pltpu.VMEM((levels, width), bf16),
            pltpu.VMEM(air_temp.shape, f32),
            pltpu.VMEM(wind_field.shape, bf16),
            pltpu.VMEM(physics.shape, f32),
            pltpu.VMEM(mixing.shape, f32),
        ),
        in_specs=[pl.BlockSpec(memory_space=pltpu.HBM)] * 4,
        out_specs=tuple(whole(7)),
        scratch_shapes=[pltpu.SemaphoreType.DMA((2, 3)), pltpu.SemaphoreType.DMA((2,))],
        compiler_params=params,
        name="pack",
    )(*(in_hbm(value) for value in (air_temp, wind_field, physics, mixing)))
    even_side, odd_side = exchange(to_even, to_odd, "cpl")

    kept = (ocean_mask, sea_surface, remap_tiles, ocean_temp)
    passing = (owner_route.reshape(1, rows), ocean_tile, shortwave, weight_tile)
    (
        ocean_mask,
        sea_surface,
        remap_tiles,
        ocean_temp,
        exchange_rate,
        sun,
        bank_near,
        start,
        wanted,
        forward,
        stack,
    ) = pl.pallas_call(
        start_kernel,
        out_shape=tuple(pltpu.VMEM(value.shape, value.dtype) for value in kept)
        + (
            shape_of((rows, width)),
            shape_of((rows, width)),
            shape_of((rows, width), jnp.int32),
            shape_of((slots, width)),
            shape_of((2 * rows, width)),
            shape_of((3 * width, remap_tiles.shape[0] * ocean_width), bf16),
            shape_of((levels, 3 * levels), bf16),
        ),
        in_specs=whole(3)
        + [pl.BlockSpec(memory_space=pl.ANY)]
        + [pl.BlockSpec(memory_space=pltpu.HBM)] * len(passing + kept),
        out_specs=tuple(whole(len(kept) + 7)),
        scratch_shapes=[pltpu.VMEM(value.shape, value.dtype) for value in passing]
        + [pltpu.SemaphoreType.DMA((len(passing + kept),))],
        compiler_params=params,
        name="start",
    )(wind_here, physics, mixing, packed, *(in_hbm(value) for value in passing + kept))

    def edge(upper, after):
        return pl.pallas_call(
            make_edge_kernel(rows, upper),
            out_shape=(shape_of((3 * levels + 16, width), bf16), shape_of((2, levels, width))),
            in_specs=whole(4) + [pl.BlockSpec(memory_space=pl.ANY)],
            out_specs=tuple(whole(2)),
            compiler_params=params,
            name="edge",
        )(air_here, wind_here, even_side, odd_side, after)

    to_high, partial_high = edge(1, start)
    below = shift(to_high, "atm", 1)
    to_low, partial_low = edge(0, partial_high)
    above = shift(to_low, "atm", -1)

    air_inner, near, bottom = pl.pallas_call(
        inner_kernel,
        out_shape=(
            pltpu.VMEM((rows, levels, width), f32),
            shape_of((4, levels, width)),
            shape_of((rows, width)),
        ),
        in_specs=whole(6),
        out_specs=tuple(whole(3)),
        scratch_shapes=[pltpu.VMEM((rows, levels, width), f32)],
        compiler_params=params,
        name="inner",
    )(air_here, wind_here, stack, packed, even_side, odd_side)

    air_edges, bottom_next, message = pl.pallas_call(
        make_outer_kernel(rows),
        out_shape=(
            shape_of((4, levels, width)),
            shape_of((rows, width)),
            shape_of((slots, width)),
        ),
        in_specs=whole(18),
        out_specs=tuple(whole(3)),
        compiler_params=params,
        name="outer",
    )(
        above,
        below,
        partial_low,
        partial_high,
        air_here,
        wind_here,
        packed,
        even_side,
        odd_side,
        near,
        stack,
        bottom,
        exchange_rate,
        sun,
        sea_surface,
        bank_near,
        forward,
        start,
    )

    if groups <= 4:
        turns = sorted(range(1, groups), key=lambda turn: abs(2 * turn - groups))
        gathered = [message] + [shift(message, "cpl", turn) for turn in turns]
    else:
        gathered = [message, lax.all_gather(message, "cpl")]

    air_next, base, response, total_weight, backward = pl.pallas_call(
        settle_kernel,
        out_shape=(
            shape_of((rows, levels, width)),
            shape_of(ocean_shape),
            shape_of((ocean_shape[0], width)),
            shape_of((rows, width)),
            shape_of((3 * remap_tiles.shape[0] * ocean_width, width), bf16),
        ),
        in_specs=whole(6),
        out_specs=tuple([pl.BlockSpec(memory_space=pltpu.HBM)] + whole(4)),
        scratch_shapes=[pltpu.SemaphoreType.DMA((3,))],
        compiler_params=params,
        name="settle",
    )(air_edges, air_inner, bank_near, remap_tiles, ocean_temp, mixing)

    ocean_next, surface_temp = pl.pallas_call(
        make_last_kernel(len(gathered)),
        out_shape=(shape_of(ocean_shape), shape_of((rows, width))),
        in_specs=whole(len(gathered) + 8),
        out_specs=(pl.BlockSpec(memory_space=pltpu.HBM),) * 2,
        scratch_shapes=[
            pltpu.VMEM(ocean_shape, f32),
            pltpu.VMEM((rows, width), f32),
            pltpu.SemaphoreType.DMA((2,)),
        ],
        compiler_params=params,
        name="last",
    )(
        *gathered,
        wanted,
        base,
        response,
        total_weight,
        bottom_next,
        ocean_mask,
        bank_near,
        backward,
    )
    return (air_next, ocean_next, surface_temp)


def solution(mesh):
    placed = (
        P("atm", None, "cpl"),
        P(None, "atm", None, "cpl"),
        P(),
        P("atm", "cpl"),
        P("atm", "cpl"),
        P("atm", "cpl"),
        P("cpl", "atm", None),
        P("cpl", "atm"),
        P("cpl", "atm"),
        P(),
        P(None, ("atm", "cpl")),
        P(),
    )
    return jax.shard_map(
        local,
        mesh=mesh,
        in_specs=placed,
        out_specs=(P("atm", None, "cpl"), P(None, ("atm", "cpl")), P("atm", "cpl")),
        check_vma=False,
    )
```

profile of v0, /device:TPU:0, one launch (start us, length us, event | category | flops | bytes accessed | tf_op | source)
XLA Modules:
  0.0 21.0 jit_solution(17365803627852790263)
XLA Ops:
  0.6 1.7 %pack.1 = (f32[64,128]{1,0:T(8,128)S(1)}, bf16[64,128]{1,0:T(8,128)(2,1)S(1)}, bf16[64,128]{1,0:T(8,128)(2,1)S(1)}, f32[24,64,128]{2,1,0:T(8,128)S(1)}, bf16[2,2...) custom-call(f32[24,64,128]{2,1,0:T(8,128)} %air.1, bf16[2,24,64,128]{3,2,1,0:T(8,128)(2,1)} %wind.1, ...), custom_call_target="tpu_custom_call" | custom-call | tf_op jit(solution)/shard_map/pack/pallas_call | solution.py:563
  2.3 0.5 %collective-permute-start = (bf16[64,128]{1,0:T(8,128)(2,1)S(1)}, bf16[64,128]{1,0:T(8,128)(2,1)S(1)}, u32[]{:S(2)}, u32[]{:S(2)}) collective-permute-start(bf16[64,128]{1,0:T(8,128)(2,1)S(1)} %get-tuple-element.40), channel_id=1, source_target_pairs={{0,1},{1,0},{2,3},{3,2},{4,5},{5,4},{6,7},{7,6},{8,9},{9,8},{10,11... | collective-permute-start | bytes 49160 | tf_op jit(solution)/shard_map/ppermute | solution.py:27
  2.8 2.6 %collective-permute-start.1 = (bf16[64,128]{1,0:T(8,128)(2,1)S(1)}, bf16[64,128]{1,0:T(8,128)(2,1)S(1)}, u32[]{:S(2)}, u32[]{:S(2)}) collective-permute-start(bf16[64,128]{1,0:T(8,128)(2,1)S(1)} %get-tuple-element.41), channel_id=1, source_target_pairs={{1,2},{3,0},{2,1},{0,3},{5,6},{7,4},{6,5},{4,7},{9,10},{11,8},{10,... | collective-permute-start | bytes 49160 | tf_op jit(solution)/shard_map/ppermute | solution.py:26
  5.5 1.6 %start.1 = (s32[24,128]{1,0:T(8,128)S(1)}, f32[24,128]{1,0:T(8,128)S(1)}, f32[16,32,128]{2,1,0:T(8,128)S(1)}, f32[80,768]{1,0:T(8,128)S(1)}, f32[24,128]{1,0:T(8...) custom-call(bf16[2,24,64,128]{3,2,1,0:T(8,128)(2,1)S(1)} %get-tuple-, ...), custom_call_target="tpu_custom_call" | custom-call | tf_op jit(solution)/shard_map/start/pallas_call | solution.py:596
  7.1 0.0 collective-permute-done.even_side
  7.1 0.0 collective-permute-done.1.odd_side
  7.1 0.1 edge.2
  7.2 1.6 %collective-permute-start.3 = (bf16[208,128]{1,0:T(8,128)(2,1)S(1)}, bf16[208,128]{1,0:T(8,128)(2,1)S(1)}, u32[]{:S(2)}, u32[]{:S(2)}) collective-permute-start(bf16[208,128]{1,0:T(8,128)(2,1)S(1)} %get-tuple-element.48), channel_id=1, source_target_pairs={{0,4},{4,8},{8,12},{12,16},{16,20},{20,24},{24,28},{28,0},{1,5},{5... | collective-permute-start | bytes 159752 | tf_op jit(solution)/shard_map/ppermute | solution.py:33
  8.8 0.1 edge.3
  8.9 3.3 %collective-permute-start.2 = (bf16[208,128]{1,0:T(8,128)(2,1)S(1)}, bf16[208,128]{1,0:T(8,128)(2,1)S(1)}, u32[]{:S(2)}, u32[]{:S(2)}) collective-permute-start(bf16[208,128]{1,0:T(8,128)(2,1)S(1)} %get-tuple-element.47), channel_id=1, source_target_pairs={{0,28},{4,0},{8,4},{12,8},{16,12},{20,16},{24,20},{28,24},{1,29},{... | collective-permute-start | bytes 159752 | tf_op jit(solution)/shard_map/ppermute | solution.py:33
  12.1 1.7 %inner.1 = (f32[24,64,128]{2,1,0:T(8,128)S(1)}, f32[4,64,128]{2,1,0:T(8,128)S(1)}, f32[24,128]{1,0:T(8,128)S(1)}) custom-call(f32[24,64,128]{2,1,0:T(8,128)S(1)} %get-tuple-element.38.air, bf16[2,24,64,128]{3,2,1,0:T(8,128)(2,1)S(1)} %get-tuple-element.39.winds.wind, bf16[64,192]{1,0:T(8,128)(2,1)S(1)} %get-tuple-element.50.stack_ref, ...), custom_call_target="tpu_custom_call" | custom-call | tf_op jit(solution)/shard_map/inner/pallas_call | solution.py:633
  13.8 0.4 %collective-permute-done.3.below_ref = bf16[208,128]{1,0:T(8,128)(2,1)S(1)} collective-permute-done((bf16[208,128]{1,0:T(8,128)(2,1)S(1)}, bf16[208,128]{1,0:T(8,128)(2,1)S(1)}, u32[]{:S(2)}, u32[]{:S(2)}) %collective-permute-start.3) | collective-permute-done | bytes 53280 | tf_op jit(solution)/shard_map/ppermute | solution.py:33
  14.2 0.0 collective-permute-done.2.above_ref
  14.2 0.9 %outer.1 = (f32[4,64,128]{2,1,0:T(8,128)S(1)}, f32[24,128]{1,0:T(8,128)S(1)}, f32[32,128]{1,0:T(8,128)S(1)}) custom-call(bf16[208,128]{1,0:T(8,128)(2,1)S(1)} %collective-permute-done.2.above_ref, bf16[208,128]{1,0:T(8,128)(2,1)S(1)} %collective-permute-done.3.below_ref, f32[2,64,128]{2,1,0:T(8,128)S(1)} %get-tuple-element.49.partial_low, ...), custom_call_target="tpu_custom_call" | custom-call | tf_op jit(solution)/shard_map/outer/pallas_call | solution.py:647
  15.1 0.9 %collective-permute-start.6 = (f32[32,128]{1,0:T(8,128)S(1)}, f32[32,128]{1,0:T(8,128)S(1)}, u32[]{:S(2)}, u32[]{:S(2)}) collective-permute-start(f32[32,128]{1,0:T(8,128)S(1)} %get-tuple-element.63.refs_0_), channel_id=1, source_target_pairs={{0,3},{1,0},{2,1},{3,2},{4,7},{5,4},{6,5},{7,6},{8,11},{9,8},{10,9... | collective-permute-start | bytes 49160 | tf_op jit(solution)/shard_map/ppermute | solution.py:33
  16.1 0.0 collective-permute-start.5
  16.1 1.1 %collective-permute-start.4 = (f32[32,128]{1,0:T(8,128)S(1)}, f32[32,128]{1,0:T(8,128)S(1)}, u32[]{:S(2)}, u32[]{:S(2)}) collective-permute-start(f32[32,128]{1,0:T(8,128)S(1)} %get-tuple-element.63.refs_0_), channel_id=1, source_target_pairs={{0,2},{1,3},{2,0},{3,1},{4,6},{5,7},{6,4},{7,5},{8,10},{9,11},{10,... | collective-permute-start | bytes 49160 | tf_op jit(solution)/shard_map/ppermute | solution.py:33
  17.2 1.0 %settle.1 = (f32[24,64,128]{2,1,0:T(8,128)}, f32[80,768]{1,0:T(8,128)S(1)}, f32[80,128]{1,0:T(8,128)S(1)}, f32[24,128]{1,0:T(8,128)S(1)}, bf16[1536,128]{1,0:T(8,128)(2,1)S(1)}) custom-call(f32[4,64,128]{2,1,0:T(8,128)S(1)} %get-tuple-element.58.edges, f32[24,64,128]{2,1,0:T(8,128)S(1)} %get-tuple-element.59.inner, ...), custom_call_target="tpu_custom_call" | custom-call | tf_op jit(solution)/shard_map/settle/pallas_call | solution.py:685
  18.2 0.0 collective-permute-done.6.refs_3_
  18.2 1.0 %collective-permute-done.5.refs_2_ = f32[32,128]{1,0:T(8,128)S(1)} collective-permute-done((f32[32,128]{1,0:T(8,128)S(1)}, f32[32,128]{1,0:T(8,128)S(1)}, u32[]{:S(2)}, u32[]{:S(2)}) %collective-permute-start.5) | collective-permute-done | bytes 16416 | tf_op jit(solution)/shard_map/ppermute | solution.py:33
  19.2 0.6 %collective-permute-done.4.refs_1_ = f32[32,128]{1,0:T(8,128)S(1)} collective-permute-done((f32[32,128]{1,0:T(8,128)S(1)}, f32[32,128]{1,0:T(8,128)S(1)}, u32[]{:S(2)}, u32[]{:S(2)}) %collective-permute-start.4) | collective-permute-done | bytes 16416 | tf_op jit(solution)/shard_map/ppermute | solution.py:33
  19.9 1.1 %last.1 = (f32[80,768]{1,0:T(8,128)}, f32[24,128]{1,0:T(8,128)}) custom-call(f32[32,128]{1,0:T(8,128)S(1)} %get-tuple-element.63.refs_0_, f32[32,128]{1,0:T(8,128)S(1)} %collective-permute-done.4.refs_1_, f32[32,128]{1,0:T(8,128)S(1)} %collective-permute-done.5.refs_2_, f32[32,128]{1,0:T(8,128)S(1)} %collective-permute-done.6.refs_3_, ...), custom_call_target="tpu_custom_call" | custom-call | tf_op jit(solution)/shard_map/last/pallas_call | solution.py:701
Async XLA Ops:
  2.3 4.7 %collective-permute-start = (bf16[64,128]{1,0:T(8,128)(2,1)S(1)}, bf16[64,128]{1,0:T(8,128)(2,1)S(1)}, u32[]{:S(2)}, u32[]{:S(2)}) collective-permute-start(bf16[64,128]{1,0:T(8,128)(2,1)S(1)} %get-tuple-element.40), channel_id=1, source_target_pairs={{0,1},{1,0},{2,3},{3,2},{4,5},{5,4},{6,7},{7,6},{8,9},{9,8},{10,11... | collective-permute-start | bytes 49160 | tf_op jit(solution)/shard_map/ppermute | solution.py:27
  2.8 4.2 %collective-permute-start.1 = (bf16[64,128]{1,0:T(8,128)(2,1)S(1)}, bf16[64,128]{1,0:T(8,128)(2,1)S(1)}, u32[]{:S(2)}, u32[]{:S(2)}) collective-permute-start(bf16[64,128]{1,0:T(8,128)(2,1)S(1)} %get-tuple-element.41), channel_id=1, source_target_pairs={{1,2},{3,0},{2,1},{0,3},{5,6},{7,4},{6,5},{4,7},{9,10},{11,8},{10,... | collective-permute-start | bytes 49160 | tf_op jit(solution)/shard_map/ppermute | solution.py:26
  7.2 7.0 %collective-permute-start.3 = (bf16[208,128]{1,0:T(8,128)(2,1)S(1)}, bf16[208,128]{1,0:T(8,128)(2,1)S(1)}, u32[]{:S(2)}, u32[]{:S(2)}) collective-permute-start(bf16[208,128]{1,0:T(8,128)(2,1)S(1)} %get-tuple-element.48), channel_id=1, source_target_pairs={{0,4},{4,8},{8,12},{12,16},{16,20},{20,24},{24,28},{28,0},{1,5},{5... | collective-permute-start | bytes 159752 | tf_op jit(solution)/shard_map/ppermute | solution.py:33
  8.9 5.4 %collective-permute-start.2 = (bf16[208,128]{1,0:T(8,128)(2,1)S(1)}, bf16[208,128]{1,0:T(8,128)(2,1)S(1)}, u32[]{:S(2)}, u32[]{:S(2)}) collective-permute-start(bf16[208,128]{1,0:T(8,128)(2,1)S(1)} %get-tuple-element.47), channel_id=1, source_target_pairs={{0,28},{4,0},{8,4},{12,8},{16,12},{20,16},{24,20},{28,24},{1,29},{... | collective-permute-start | bytes 159752 | tf_op jit(solution)/shard_map/ppermute | solution.py:33
  15.1 3.1 %collective-permute-start.6 = (f32[32,128]{1,0:T(8,128)S(1)}, f32[32,128]{1,0:T(8,128)S(1)}, u32[]{:S(2)}, u32[]{:S(2)}) collective-permute-start(f32[32,128]{1,0:T(8,128)S(1)} %get-tuple-element.63.refs_0_), channel_id=1, source_target_pairs={{0,3},{1,0},{2,1},{3,2},{4,7},{5,4},{6,5},{7,6},{8,11},{9,8},{10,9... | collective-permute-start | bytes 49160 | tf_op jit(solution)/shard_map/ppermute | solution.py:33
  16.1 3.2 %collective-permute-start.5 = (f32[32,128]{1,0:T(8,128)S(1)}, f32[32,128]{1,0:T(8,128)S(1)}, u32[]{:S(2)}, u32[]{:S(2)}) collective-permute-start(f32[32,128]{1,0:T(8,128)S(1)} %get-tuple-element.63.refs_0_), channel_id=1, source_target_pairs={{0,1},{1,2},{2,3},{3,0},{4,5},{5,6},{6,7},{7,4},{8,9},{9,10},{10,1... | collective-permute-start | bytes 49160 | tf_op jit(solution)/shard_map/ppermute | solution.py:33
  16.1 3.8 %collective-permute-start.4 = (f32[32,128]{1,0:T(8,128)S(1)}, f32[32,128]{1,0:T(8,128)S(1)}, u32[]{:S(2)}, u32[]{:S(2)}) collective-permute-start(f32[32,128]{1,0:T(8,128)S(1)} %get-tuple-element.63.refs_0_), channel_id=1, source_target_pairs={{0,2},{1,3},{2,0},{3,1},{4,6},{5,7},{6,4},{7,5},{8,10},{9,11},{10,... | collective-permute-start | bytes 49160 | tf_op jit(solution)/shard_map/ppermute | solution.py:33
where the time goes:
time: 21.1 us; the launch traced here: 21 us
  starting transfers between devices  10 us (47%)
  Pallas kernels  8.19 us (39%)
  waiting for transfers between devices  2.06 us (10%)
  between operations  0.71 us (3%)
    ppermute x5, starting transfers between devices, shift(): lax.ppermute(block, axis, [(i, (i + turn) % count) for i in range(count)])  6.88 us
    ppermute x1, starting transfers between devices, exchange(): odd_side = lax.ppermute(to_odd, axis, pair_odd(count))  2.61 us
    ppermute x5, waiting for transfers between devices, shift(): lax.ppermute(block, axis, [(i, (i + turn) % count) for i in range(count)])  2.05 us
    pallas_call x1, Pallas kernels, local(): pl.pallas_call(pack_kernel, out_shape=(pltpu.VMEM((levels, width), f32),...  1.68 us
    pallas_call x1, Pallas kernels, local(): pl.pallas_call(inner_kernel, out_shape=(pltpu.VMEM((rows, levels, width),...  1.67 us
    pallas_call x1, Pallas kernels, local(): pl.pallas_call(start_kernel, out_shape=tuple((pltpu.VMEM(value.shape, val...  1.6 us
    pallas_call x1, Pallas kernels, local(): pl.pallas_call(make_last_kernel(len(gathered)), out_shape=(shape_of(ocean...  1.12 us
    pallas_call x1, Pallas kernels, local(): pl.pallas_call(settle_kernel, out_shape=(shape_of((rows, levels, width)),...  1.02 us
  transfers between devices with their start and end apart: 7, of which 3 were waited for; matrix products, arithmetic and copies ran while one was open for 0% of the time, Pallas kernels for 21%

commit v1 on v0

--- a/solution.py
+++ b/solution.py
@@ -259,11 +259,10 @@
 
 
 def fold(value, size):
-    span = value.shape[1] // 2
-    while span >= size:
-        value = value + roll(value, span)
-        span //= 2
-    return value
+    parts = [value] + [roll(value, at) for at in range(size, value.shape[1], size)]
+    while len(parts) > 1:
+        parts = [left + right for left, right in zip(parts[0::2], parts[1::2])]
+    return parts[0]
 
 
 def chosen_shares(fluxes, halves, bank, ocean_width):

time: 21.1 us -> 21 us (level)
  Pallas kernels: 8.19 us -> 7.97 us
where the time goes in v1:
time: 21 us; the launch traced here: 20.8 us
  starting transfers between devices  10 us (48%)
  Pallas kernels  7.97 us (38%)
  waiting for transfers between devices  2.12 us (10%)
  between operations  0.71 us (3%)
    ppermute x5, starting transfers between devices, shift(): lax.ppermute(block, axis, [(i, (i + turn) % count) for i in range(count)])  6.88 us
    ppermute x1, starting transfers between devices, exchange(): odd_side = lax.ppermute(to_odd, axis, pair_odd(count))  2.61 us
    ppermute x5, waiting for transfers between devices, shift(): lax.ppermute(block, axis, [(i, (i + turn) % count) for i in range(count)])  2.12 us
    pallas_call x1, Pallas kernels, local(): pl.pallas_call(pack_kernel, out_shape=(pltpu.VMEM((levels, width), f32),...  1.68 us
    pallas_call x1, Pallas kernels, local(): pl.pallas_call(inner_kernel, out_shape=(pltpu.VMEM((rows, levels, width),...  1.67 us
    pallas_call x1, Pallas kernels, local(): pl.pallas_call(start_kernel, out_shape=tuple((pltpu.VMEM(value.shape, val...  1.54 us
    pallas_call x1, Pallas kernels, local(): pl.pallas_call(settle_kernel, out_shape=(shape_of((rows, levels, width)),...  1.02 us
    pallas_call x1, Pallas kernels, local(): pl.pallas_call(make_last_kernel(len(gathered)), out_shape=(shape_of(ocean...  1.02 us
  transfers between devices with their start and end apart: 7, of which 3 were waited for; matrix products, arithmetic and copies ran while one was open for 0% of the time, Pallas kernels for 21%

profile of v1, /device:TPU:0, one launch (start us, length us, event | category | flops | bytes accessed | tf_op | source)
XLA Modules:
  0.0 20.8 jit_solution(9341752709283928230)
XLA Ops:
  0.6 1.7 %pack.1 = (f32[64,128]{1,0:T(8,128)S(1)}, bf16[64,128]{1,0:T(8,128)(2,1)S(1)}, bf16[64,128]{1,0:T(8,128)(2,1)S(1)}, f32[24,64,128]{2,1,0:T(8,128)S(1)}, bf16[2,2...) custom-call(f32[24,64,128]{2,1,0:T(8,128)} %air.1, bf16[2,24,64,128]{3,2,1,0:T(8,128)(2,1)} %wind.1, ...), custom_call_target="tpu_custom_call" | custom-call | tf_op jit(solution)/shard_map/pack/pallas_call | solution.py:562
  2.3 0.5 %collective-permute-start = (bf16[64,128]{1,0:T(8,128)(2,1)S(1)}, bf16[64,128]{1,0:T(8,128)(2,1)S(1)}, u32[]{:S(2)}, u32[]{:S(2)}) collective-permute-start(bf16[64,128]{1,0:T(8,128)(2,1)S(1)} %get-tuple-element.40), channel_id=1, source_target_pairs={{0,1},{1,0},{2,3},{3,2},{4,5},{5,4},{6,7},{7,6},{8,9},{9,8},{10,11... | collective-permute-start | bytes 49160 | tf_op jit(solution)/shard_map/ppermute | solution.py:27
  2.8 2.6 %collective-permute-start.1 = (bf16[64,128]{1,0:T(8,128)(2,1)S(1)}, bf16[64,128]{1,0:T(8,128)(2,1)S(1)}, u32[]{:S(2)}, u32[]{:S(2)}) collective-permute-start(bf16[64,128]{1,0:T(8,128)(2,1)S(1)} %get-tuple-element.41), channel_id=1, source_target_pairs={{1,2},{3,0},{2,1},{0,3},{5,6},{7,4},{6,5},{4,7},{9,10},{11,8},{10,... | collective-permute-start | bytes 49160 | tf_op jit(solution)/shard_map/ppermute | solution.py:26
  5.5 1.5 %start.1 = (s32[24,128]{1,0:T(8,128)S(1)}, f32[24,128]{1,0:T(8,128)S(1)}, f32[16,32,128]{2,1,0:T(8,128)S(1)}, f32[80,768]{1,0:T(8,128)S(1)}, f32[24,128]{1,0:T(8...) custom-call(bf16[2,24,64,128]{3,2,1,0:T(8,128)(2,1)S(1)} %get-tuple-, ...), custom_call_target="tpu_custom_call" | custom-call | tf_op jit(solution)/shard_map/start/pallas_call | solution.py:595
  7.0 0.0 collective-permute-done.even_side
  7.0 0.0 collective-permute-done.1.odd_side
  7.0 0.1 edge.2
  7.1 1.6 %collective-permute-start.3 = (bf16[208,128]{1,0:T(8,128)(2,1)S(1)}, bf16[208,128]{1,0:T(8,128)(2,1)S(1)}, u32[]{:S(2)}, u32[]{:S(2)}) collective-permute-start(bf16[208,128]{1,0:T(8,128)(2,1)S(1)} %get-tuple-element.48), channel_id=1, source_target_pairs={{0,4},{4,8},{8,12},{12,16},{16,20},{20,24},{24,28},{28,0},{1,5},{5... | collective-permute-start | bytes 159752 | tf_op jit(solution)/shard_map/ppermute | solution.py:33
  8.8 0.1 edge.3
  8.9 3.2 %collective-permute-start.2 = (bf16[208,128]{1,0:T(8,128)(2,1)S(1)}, bf16[208,128]{1,0:T(8,128)(2,1)S(1)}, u32[]{:S(2)}, u32[]{:S(2)}) collective-permute-start(bf16[208,128]{1,0:T(8,128)(2,1)S(1)} %get-tuple-element.47), channel_id=1, source_target_pairs={{0,28},{4,0},{8,4},{12,8},{16,12},{20,16},{24,20},{28,24},{1,29},{... | collective-permute-start | bytes 159752 | tf_op jit(solution)/shard_map/ppermute | solution.py:33
  12.1 1.7 %inner.1 = (f32[24,64,128]{2,1,0:T(8,128)S(1)}, f32[4,64,128]{2,1,0:T(8,128)S(1)}, f32[24,128]{1,0:T(8,128)S(1)}) custom-call(f32[24,64,128]{2,1,0:T(8,128)S(1)} %get-tuple-element.38.air, bf16[2,24,64,128]{3,2,1,0:T(8,128)(2,1)S(1)} %get-tuple-element.39.winds.wind, bf16[64,192]{1,0:T(8,128)(2,1)S(1)} %get-tuple-element.50.stack_ref, ...), custom_call_target="tpu_custom_call" | custom-call | tf_op jit(solution)/shard_map/inner/pallas_call | solution.py:632
  13.7 0.5 %collective-permute-done.3.below_ref = bf16[208,128]{1,0:T(8,128)(2,1)S(1)} collective-permute-done((bf16[208,128]{1,0:T(8,128)(2,1)S(1)}, bf16[208,128]{1,0:T(8,128)(2,1)S(1)}, u32[]{:S(2)}, u32[]{:S(2)}) %collective-permute-start.3) | collective-permute-done | bytes 53280 | tf_op jit(solution)/shard_map/ppermute | solution.py:33
  14.2 0.0 collective-permute-done.2.above_ref
  14.2 0.8 %outer.1 = (f32[4,64,128]{2,1,0:T(8,128)S(1)}, f32[24,128]{1,0:T(8,128)S(1)}, f32[32,128]{1,0:T(8,128)S(1)}) custom-call(bf16[208,128]{1,0:T(8,128)(2,1)S(1)} %collective-permute-done.2.above_ref, bf16[208,128]{1,0:T(8,128)(2,1)S(1)} %collective-permute-done.3.below_ref, f32[2,64,128]{2,1,0:T(8,128)S(1)} %get-tuple-element.49.partial_low, ...), custom_call_target="tpu_custom_call" | custom-call | tf_op jit(solution)/shard_map/outer/pallas_call | solution.py:646
  15.1 0.9 %collective-permute-start.6 = (f32[32,128]{1,0:T(8,128)S(1)}, f32[32,128]{1,0:T(8,128)S(1)}, u32[]{:S(2)}, u32[]{:S(2)}) collective-permute-start(f32[32,128]{1,0:T(8,128)S(1)} %get-tuple-element.63.refs_0_), channel_id=1, source_target_pairs={{0,3},{1,0},{2,1},{3,2},{4,7},{5,4},{6,5},{7,6},{8,11},{9,8},{10,9... | collective-permute-start | bytes 49160 | tf_op jit(solution)/shard_map/ppermute | solution.py:33
  16.0 0.0 collective-permute-start.5
  16.0 1.1 %collective-permute-start.4 = (f32[32,128]{1,0:T(8,128)S(1)}, f32[32,128]{1,0:T(8,128)S(1)}, u32[]{:S(2)}, u32[]{:S(2)}) collective-permute-start(f32[32,128]{1,0:T(8,128)S(1)} %get-tuple-element.63.refs_0_), channel_id=1, source_target_pairs={{0,2},{1,3},{2,0},{3,1},{4,6},{5,7},{6,4},{7,5},{8,10},{9,11},{10,... | collective-permute-start | bytes 49160 | tf_op jit(solution)/shard_map/ppermute | solution.py:33
  17.1 1.0 %settle.1 = (f32[24,64,128]{2,1,0:T(8,128)}, f32[80,768]{1,0:T(8,128)S(1)}, f32[80,128]{1,0:T(8,128)S(1)}, f32[24,128]{1,0:T(8,128)S(1)}, bf16[1536,128]{1,0:T(8,128)(2,1)S(1)}) custom-call(f32[4,64,128]{2,1,0:T(8,128)S(1)} %get-tuple-element.58.edges, f32[24,64,128]{2,1,0:T(8,128)S(1)} %get-tuple-element.59.inner, ...), custom_call_target="tpu_custom_call" | custom-call | tf_op jit(solution)/shard_map/settle/pallas_call | solution.py:684
  18.2 0.0 collective-permute-done.6.refs_3_
  18.2 1.0 %collective-permute-done.5.refs_2_ = f32[32,128]{1,0:T(8,128)S(1)} collective-permute-done((f32[32,128]{1,0:T(8,128)S(1)}, f32[32,128]{1,0:T(8,128)S(1)}, u32[]{:S(2)}, u32[]{:S(2)}) %collective-permute-start.5) | collective-permute-done | bytes 16416 | tf_op jit(solution)/shard_map/ppermute | solution.py:33
  19.2 0.6 %collective-permute-done.4.refs_1_ = f32[32,128]{1,0:T(8,128)S(1)} collective-permute-done((f32[32,128]{1,0:T(8,128)S(1)}, f32[32,128]{1,0:T(8,128)S(1)}, u32[]{:S(2)}, u32[]{:S(2)}) %collective-permute-start.4) | collective-permute-done | bytes 16416 | tf_op jit(solution)/shard_map/ppermute | solution.py:33
  19.8 1.0 %last.1 = (f32[80,768]{1,0:T(8,128)}, f32[24,128]{1,0:T(8,128)}) custom-call(f32[32,128]{1,0:T(8,128)S(1)} %get-tuple-element.63.refs_0_, f32[32,128]{1,0:T(8,128)S(1)} %collective-permute-done.4.refs_1_, f32[32,128]{1,0:T(8,128)S(1)} %collective-permute-done.5.refs_2_, f32[32,128]{1,0:T(8,128)S(1)} %collective-permute-done.6.refs_3_, ...), custom_call_target="tpu_custom_call" | custom-call | tf_op jit(solution)/shard_map/last/pallas_call | solution.py:700
Async XLA Ops:
  2.3 4.7 %collective-permute-start = (bf16[64,128]{1,0:T(8,128)(2,1)S(1)}, bf16[64,128]{1,0:T(8,128)(2,1)S(1)}, u32[]{:S(2)}, u32[]{:S(2)}) collective-permute-start(bf16[64,128]{1,0:T(8,128)(2,1)S(1)} %get-tuple-element.40), channel_id=1, source_target_pairs={{0,1},{1,0},{2,3},{3,2},{4,5},{5,4},{6,7},{7,6},{8,9},{9,8},{10,11... | collective-permute-start | bytes 49160 | tf_op jit(solution)/shard_map/ppermute | solution.py:27
  2.8 4.2 %collective-permute-start.1 = (bf16[64,128]{1,0:T(8,128)(2,1)S(1)}, bf16[64,128]{1,0:T(8,128)(2,1)S(1)}, u32[]{:S(2)}, u32[]{:S(2)}) collective-permute-start(bf16[64,128]{1,0:T(8,128)(2,1)S(1)} %get-tuple-element.41), channel_id=1, source_target_pairs={{1,2},{3,0},{2,1},{0,3},{5,6},{7,4},{6,5},{4,7},{9,10},{11,8},{10,... | collective-permute-start | bytes 49160 | tf_op jit(solution)/shard_map/ppermute | solution.py:26
  7.1 7.1 %collective-permute-start.3 = (bf16[208,128]{1,0:T(8,128)(2,1)S(1)}, bf16[208,128]{1,0:T(8,128)(2,1)S(1)}, u32[]{:S(2)}, u32[]{:S(2)}) collective-permute-start(bf16[208,128]{1,0:T(8,128)(2,1)S(1)} %get-tuple-element.48), channel_id=1, source_target_pairs={{0,4},{4,8},{8,12},{12,16},{16,20},{20,24},{24,28},{28,0},{1,5},{5... | collective-permute-start | bytes 159752 | tf_op jit(solution)/shard_map/ppermute | solution.py:33
  8.9 5.4 %collective-permute-start.2 = (bf16[208,128]{1,0:T(8,128)(2,1)S(1)}, bf16[208,128]{1,0:T(8,128)(2,1)S(1)}, u32[]{:S(2)}, u32[]{:S(2)}) collective-permute-start(bf16[208,128]{1,0:T(8,128)(2,1)S(1)} %get-tuple-element.47), channel_id=1, source_target_pairs={{0,28},{4,0},{8,4},{12,8},{16,12},{20,16},{24,20},{28,24},{1,29},{... | collective-permute-start | bytes 159752 | tf_op jit(solution)/shard_map/ppermute | solution.py:33
  15.1 3.1 %collective-permute-start.6 = (f32[32,128]{1,0:T(8,128)S(1)}, f32[32,128]{1,0:T(8,128)S(1)}, u32[]{:S(2)}, u32[]{:S(2)}) collective-permute-start(f32[32,128]{1,0:T(8,128)S(1)} %get-tuple-element.63.refs_0_), channel_id=1, source_target_pairs={{0,3},{1,0},{2,1},{3,2},{4,7},{5,4},{6,5},{7,6},{8,11},{9,8},{10,9... | collective-permute-start | bytes 49160 | tf_op jit(solution)/shard_map/ppermute | solution.py:33
  16.0 3.2 %collective-permute-start.5 = (f32[32,128]{1,0:T(8,128)S(1)}, f32[32,128]{1,0:T(8,128)S(1)}, u32[]{:S(2)}, u32[]{:S(2)}) collective-permute-start(f32[32,128]{1,0:T(8,128)S(1)} %get-tuple-element.63.refs_0_), channel_id=1, source_target_pairs={{0,1},{1,2},{2,3},{3,0},{4,5},{5,6},{6,7},{7,4},{8,9},{9,10},{10,1... | collective-permute-start | bytes 49160 | tf_op jit(solution)/shard_map/ppermute | solution.py:33
  16.0 3.8 %collective-permute-start.4 = (f32[32,128]{1,0:T(8,128)S(1)}, f32[32,128]{1,0:T(8,128)S(1)}, u32[]{:S(2)}, u32[]{:S(2)}) collective-permute-start(f32[32,128]{1,0:T(8,128)S(1)} %get-tuple-element.63.refs_0_), channel_id=1, source_target_pairs={{0,2},{1,3},{2,0},{3,1},{4,6},{5,7},{6,4},{7,5},{8,10},{9,11},{10,... | collective-permute-start | bytes 49160 | tf_op jit(solution)/shard_map/ppermute | solution.py:33

commit v2 on v1

--- a/solution.py
+++ b/solution.py
@@ -84,8 +84,6 @@
         pltpu.make_async_copy(physics, physics_here, square_sems.at[0]),
         pltpu.make_async_copy(mixing, mixing_here, square_sems.at[1]),
     ]
-    for copy in squares:
-        copy.start()
     parts = sems.shape[1]
     size = rows // parts
     copies = []
@@ -99,6 +97,8 @@
         )
         for copy in copies[-1]:
             copy.start()
+    for copy in squares:
+        copy.start()
     cells = jnp.zeros((levels, width), bf16)
     first = jnp.zeros((levels, width), bf16)
     second = jnp.zeros((levels, width), bf16)
@@ -478,10 +478,9 @@
             for at in range(0, len(labels), 2)
         ]
         high, low = split(jnp.concatenate(values, axis=0))
-        got = jnp.dot(
-            jnp.concatenate(hot + hot, axis=1),
-            jnp.concatenate([high, low], axis=0),
-            preferred_element_type=f32,
+        marks = jnp.concatenate(hot, axis=1)
+        got = jnp.dot(marks, high, preferred_element_type=f32) + jnp.dot(
+            marks, low, preferred_element_type=f32
         )
         near = iota((rows, width), 1)
         seen = fold(jnp.where(near >= 2 * ocean_width, got[0:rows], 0.0), ocean_width)

time: 21 us -> 21 us (level)
  no operation moved by 1% of the time
where the time goes in v2:
time: 21 us; the launch traced here: 20.8 us
  starting transfers between devices  10 us (48%)
  Pallas kernels  7.96 us (38%)
  waiting for transfers between devices  2.12 us (10%)
  between operations  0.71 us (3%)
    ppermute x5, starting transfers between devices, shift(): lax.ppermute(block, axis, [(i, (i + turn) % count) for i in range(count)])  6.88 us
    ppermute x1, starting transfers between devices, exchange(): odd_side = lax.ppermute(to_odd, axis, pair_odd(count))  2.61 us
    ppermute x5, waiting for transfers between devices, shift(): lax.ppermute(block, axis, [(i, (i + turn) % count) for i in range(count)])  2.11 us
    pallas_call x1, Pallas kernels, local(): pl.pallas_call(pack_kernel, out_shape=(pltpu.VMEM((levels, width), f32),...  1.68 us
    pallas_call x1, Pallas kernels, local(): pl.pallas_call(inner_kernel, out_shape=(pltpu.VMEM((rows, levels, width),...  1.67 us
    pallas_call x1, Pallas kernels, local(): pl.pallas_call(start_kernel, out_shape=tuple((pltpu.VMEM(value.shape, val...  1.54 us
    pallas_call x1, Pallas kernels, local(): pl.pallas_call(settle_kernel, out_shape=(shape_of((rows, levels, width)),...  1.03 us
    pallas_call x1, Pallas kernels, local(): pl.pallas_call(make_last_kernel(len(gathered)), out_shape=(shape_of(ocean...  1.02 us
  transfers between devices with their start and end apart: 7, of which 3 were waited for; matrix products, arithmetic and copies ran while one was open for 0% of the time, Pallas kernels for 21%

profile of v2, /device:TPU:0, one launch (start us, length us, event | category | flops | bytes accessed | tf_op | source)
XLA Modules:
  0.0 20.8 jit_solution(11499868229724451562)
XLA Ops:
  0.6 1.7 %pack.1 = (f32[64,128]{1,0:T(8,128)S(1)}, bf16[64,128]{1,0:T(8,128)(2,1)S(1)}, bf16[64,128]{1,0:T(8,128)(2,1)S(1)}, f32[24,64,128]{2,1,0:T(8,128)S(1)}, bf16[2,2...) custom-call(f32[24,64,128]{2,1,0:T(8,128)} %air.1, bf16[2,24,64,128]{3,2,1,0:T(8,128)(2,1)} %wind.1, ...), custom_call_target="tpu_custom_call" | custom-call | tf_op jit(solution)/shard_map/pack/pallas_call | solution.py:561
  2.3 0.5 %collective-permute-start = (bf16[64,128]{1,0:T(8,128)(2,1)S(1)}, bf16[64,128]{1,0:T(8,128)(2,1)S(1)}, u32[]{:S(2)}, u32[]{:S(2)}) collective-permute-start(bf16[64,128]{1,0:T(8,128)(2,1)S(1)} %get-tuple-element.40), channel_id=1, source_target_pairs={{0,1},{1,0},{2,3},{3,2},{4,5},{5,4},{6,7},{7,6},{8,9},{9,8},{10,11... | collective-permute-start | bytes 49160 | tf_op jit(solution)/shard_map/ppermute | solution.py:27
  2.8 2.6 %collective-permute-start.1 = (bf16[64,128]{1,0:T(8,128)(2,1)S(1)}, bf16[64,128]{1,0:T(8,128)(2,1)S(1)}, u32[]{:S(2)}, u32[]{:S(2)}) collective-permute-start(bf16[64,128]{1,0:T(8,128)(2,1)S(1)} %get-tuple-element.41), channel_id=1, source_target_pairs={{1,2},{3,0},{2,1},{0,3},{5,6},{7,4},{6,5},{4,7},{9,10},{11,8},{10,... | collective-permute-start | bytes 49160 | tf_op jit(solution)/shard_map/ppermute | solution.py:26
  5.5 1.5 %start.1 = (s32[24,128]{1,0:T(8,128)S(1)}, f32[24,128]{1,0:T(8,128)S(1)}, f32[16,32,128]{2,1,0:T(8,128)S(1)}, f32[80,768]{1,0:T(8,128)S(1)}, f32[24,128]{1,0:T(8...) custom-call(bf16[2,24,64,128]{3,2,1,0:T(8,128)(2,1)S(1)} %get-tuple-, ...), custom_call_target="tpu_custom_call" | custom-call | tf_op jit(solution)/shard_map/start/pallas_call | solution.py:594
  7.0 0.0 collective-permute-done.even_side
  7.0 0.0 collective-permute-done.1.odd_side
  7.0 0.1 edge.2
  7.1 1.6 %collective-permute-start.3 = (bf16[208,128]{1,0:T(8,128)(2,1)S(1)}, bf16[208,128]{1,0:T(8,128)(2,1)S(1)}, u32[]{:S(2)}, u32[]{:S(2)}) collective-permute-start(bf16[208,128]{1,0:T(8,128)(2,1)S(1)} %get-tuple-element.48), channel_id=1, source_target_pairs={{0,4},{4,8},{8,12},{12,16},{16,20},{20,24},{24,28},{28,0},{1,5},{5... | collective-permute-start | bytes 159752 | tf_op jit(solution)/shard_map/ppermute | solution.py:33
  8.8 0.1 edge.3
  8.9 3.2 %collective-permute-start.2 = (bf16[208,128]{1,0:T(8,128)(2,1)S(1)}, bf16[208,128]{1,0:T(8,128)(2,1)S(1)}, u32[]{:S(2)}, u32[]{:S(2)}) collective-permute-start(bf16[208,128]{1,0:T(8,128)(2,1)S(1)} %get-tuple-element.47), channel_id=1, source_target_pairs={{0,28},{4,0},{8,4},{12,8},{16,12},{20,16},{24,20},{28,24},{1,29},{... | collective-permute-start | bytes 159752 | tf_op jit(solution)/shard_map/ppermute | solution.py:33
  12.1 1.7 %inner.1 = (f32[24,64,128]{2,1,0:T(8,128)S(1)}, f32[4,64,128]{2,1,0:T(8,128)S(1)}, f32[24,128]{1,0:T(8,128)S(1)}) custom-call(f32[24,64,128]{2,1,0:T(8,128)S(1)} %get-tuple-element.38.air, bf16[2,24,64,128]{3,2,1,0:T(8,128)(2,1)S(1)} %get-tuple-element.39.winds.wind, bf16[64,192]{1,0:T(8,128)(2,1)S(1)} %get-tuple-element.50.stack_ref, ...), custom_call_target="tpu_custom_call" | custom-call | tf_op jit(solution)/shard_map/inner/pallas_call | solution.py:631
  13.7 0.5 %collective-permute-done.3.below_ref = bf16[208,128]{1,0:T(8,128)(2,1)S(1)} collective-permute-done((bf16[208,128]{1,0:T(8,128)(2,1)S(1)}, bf16[208,128]{1,0:T(8,128)(2,1)S(1)}, u32[]{:S(2)}, u32[]{:S(2)}) %collective-permute-start.3) | collective-permute-done | bytes 53280 | tf_op jit(solution)/shard_map/ppermute | solution.py:33
  14.2 0.0 collective-permute-done.2.above_ref
  14.2 0.8 %outer.1 = (f32[4,64,128]{2,1,0:T(8,128)S(1)}, f32[24,128]{1,0:T(8,128)S(1)}, f32[32,128]{1,0:T(8,128)S(1)}) custom-call(bf16[208,128]{1,0:T(8,128)(2,1)S(1)} %collective-permute-done.2.above_ref, bf16[208,128]{1,0:T(8,128)(2,1)S(1)} %collective-permute-done.3.below_ref, f32[2,64,128]{2,1,0:T(8,128)S(1)} %get-tuple-element.49.partial_low, ...), custom_call_target="tpu_custom_call" | custom-call | tf_op jit(solution)/shard_map/outer/pallas_call | solution.py:645
  15.1 0.9 %collective-permute-start.6 = (f32[32,128]{1,0:T(8,128)S(1)}, f32[32,128]{1,0:T(8,128)S(1)}, u32[]{:S(2)}, u32[]{:S(2)}) collective-permute-start(f32[32,128]{1,0:T(8,128)S(1)} %get-tuple-element.63.refs_0_), channel_id=1, source_target_pairs={{0,3},{1,0},{2,1},{3,2},{4,7},{5,4},{6,5},{7,6},{8,11},{9,8},{10,9... | collective-permute-start | bytes 49160 | tf_op jit(solution)/shard_map/ppermute | solution.py:33
  16.0 0.0 collective-permute-start.5
  16.0 1.1 %collective-permute-start.4 = (f32[32,128]{1,0:T(8,128)S(1)}, f32[32,128]{1,0:T(8,128)S(1)}, u32[]{:S(2)}, u32[]{:S(2)}) collective-permute-start(f32[32,128]{1,0:T(8,128)S(1)} %get-tuple-element.63.refs_0_), channel_id=1, source_target_pairs={{0,2},{1,3},{2,0},{3,1},{4,6},{5,7},{6,4},{7,5},{8,10},{9,11},{10,... | collective-permute-start | bytes 49160 | tf_op jit(solution)/shard_map/ppermute | solution.py:33
  17.1 1.0 %settle.1 = (f32[24,64,128]{2,1,0:T(8,128)}, f32[80,768]{1,0:T(8,128)S(1)}, f32[80,128]{1,0:T(8,128)S(1)}, f32[24,128]{1,0:T(8,128)S(1)}, bf16[1536,128]{1,0:T(8,128)(2,1)S(1)}) custom-call(f32[4,64,128]{2,1,0:T(8,128)S(1)} %get-tuple-element.58.edges, f32[24,64,128]{2,1,0:T(8,128)S(1)} %get-tuple-element.59.inner, ...), custom_call_target="tpu_custom_call" | custom-call | tf_op jit(solution)/shard_map/settle/pallas_call | solution.py:683
  18.2 0.0 collective-permute-done.6.refs_3_
  18.2 1.0 %collective-permute-done.5.refs_2_ = f32[32,128]{1,0:T(8,128)S(1)} collective-permute-done((f32[32,128]{1,0:T(8,128)S(1)}, f32[32,128]{1,0:T(8,128)S(1)}, u32[]{:S(2)}, u32[]{:S(2)}) %collective-permute-start.5) | collective-permute-done | bytes 16416 | tf_op jit(solution)/shard_map/ppermute | solution.py:33
  19.2 0.6 %collective-permute-done.4.refs_1_ = f32[32,128]{1,0:T(8,128)S(1)} collective-permute-done((f32[32,128]{1,0:T(8,128)S(1)}, f32[32,128]{1,0:T(8,128)S(1)}, u32[]{:S(2)}, u32[]{:S(2)}) %collective-permute-start.4) | collective-permute-done | bytes 16416 | tf_op jit(solution)/shard_map/ppermute | solution.py:33
  19.8 1.0 %last.1 = (f32[80,768]{1,0:T(8,128)}, f32[24,128]{1,0:T(8,128)}) custom-call(f32[32,128]{1,0:T(8,128)S(1)} %get-tuple-element.63.refs_0_, f32[32,128]{1,0:T(8,128)S(1)} %collective-permute-done.4.refs_1_, f32[32,128]{1,0:T(8,128)S(1)} %collective-permute-done.5.refs_2_, f32[32,128]{1,0:T(8,128)S(1)} %collective-permute-done.6.refs_3_, ...), custom_call_target="tpu_custom_call" | custom-call | tf_op jit(solution)/shard_map/last/pallas_call | solution.py:699
Async XLA Ops:
  2.3 4.7 %collective-permute-start = (bf16[64,128]{1,0:T(8,128)(2,1)S(1)}, bf16[64,128]{1,0:T(8,128)(2,1)S(1)}, u32[]{:S(2)}, u32[]{:S(2)}) collective-permute-start(bf16[64,128]{1,0:T(8,128)(2,1)S(1)} %get-tuple-element.40), channel_id=1, source_target_pairs={{0,1},{1,0},{2,3},{3,2},{4,5},{5,4},{6,7},{7,6},{8,9},{9,8},{10,11... | collective-permute-start | bytes 49160 | tf_op jit(solution)/shard_map/ppermute | solution.py:27
  2.8 4.2 %collective-permute-start.1 = (bf16[64,128]{1,0:T(8,128)(2,1)S(1)}, bf16[64,128]{1,0:T(8,128)(2,1)S(1)}, u32[]{:S(2)}, u32[]{:S(2)}) collective-permute-start(bf16[64,128]{1,0:T(8,128)(2,1)S(1)} %get-tuple-element.41), channel_id=1, source_target_pairs={{1,2},{3,0},{2,1},{0,3},{5,6},{7,4},{6,5},{4,7},{9,10},{11,8},{10,... | collective-permute-start | bytes 49160 | tf_op jit(solution)/shard_map/ppermute | solution.py:26
  7.1 7.1 %collective-permute-start.3 = (bf16[208,128]{1,0:T(8,128)(2,1)S(1)}, bf16[208,128]{1,0:T(8,128)(2,1)S(1)}, u32[]{:S(2)}, u32[]{:S(2)}) collective-permute-start(bf16[208,128]{1,0:T(8,128)(2,1)S(1)} %get-tuple-element.48), channel_id=1, source_target_pairs={{0,4},{4,8},{8,12},{12,16},{16,20},{20,24},{24,28},{28,0},{1,5},{5... | collective-permute-start | bytes 159752 | tf_op jit(solution)/shard_map/ppermute | solution.py:33
  8.9 5.4 %collective-permute-start.2 = (bf16[208,128]{1,0:T(8,128)(2,1)S(1)}, bf16[208,128]{1,0:T(8,128)(2,1)S(1)}, u32[]{:S(2)}, u32[]{:S(2)}) collective-permute-start(bf16[208,128]{1,0:T(8,128)(2,1)S(1)} %get-tuple-element.47), channel_id=1, source_target_pairs={{0,28},{4,0},{8,4},{12,8},{16,12},{20,16},{24,20},{28,24},{1,29},{... | collective-permute-start | bytes 159752 | tf_op jit(solution)/shard_map/ppermute | solution.py:33
  15.1 3.1 %collective-permute-start.6 = (f32[32,128]{1,0:T(8,128)S(1)}, f32[32,128]{1,0:T(8,128)S(1)}, u32[]{:S(2)}, u32[]{:S(2)}) collective-permute-start(f32[32,128]{1,0:T(8,128)S(1)} %get-tuple-element.63.refs_0_), channel_id=1, source_target_pairs={{0,3},{1,0},{2,1},{3,2},{4,7},{5,4},{6,5},{7,6},{8,11},{9,8},{10,9... | collective-permute-start | bytes 49160 | tf_op jit(solution)/shard_map/ppermute | solution.py:33
  16.0 3.2 %collective-permute-start.5 = (f32[32,128]{1,0:T(8,128)S(1)}, f32[32,128]{1,0:T(8,128)S(1)}, u32[]{:S(2)}, u32[]{:S(2)}) collective-permute-start(f32[32,128]{1,0:T(8,128)S(1)} %get-tuple-element.63.refs_0_), channel_id=1, source_target_pairs={{0,1},{1,2},{2,3},{3,0},{4,5},{5,6},{6,7},{7,4},{8,9},{9,10},{10,1... | collective-permute-start | bytes 49160 | tf_op jit(solution)/shard_map/ppermute | solution.py:33
  16.0 3.8 %collective-permute-start.4 = (f32[32,128]{1,0:T(8,128)S(1)}, f32[32,128]{1,0:T(8,128)S(1)}, u32[]{:S(2)}, u32[]{:S(2)}) collective-permute-start(f32[32,128]{1,0:T(8,128)S(1)} %get-tuple-element.63.refs_0_), channel_id=1, source_target_pairs={{0,2},{1,3},{2,0},{3,1},{4,6},{5,7},{6,4},{7,5},{8,10},{9,11},{10,... | collective-permute-start | bytes 49160 | tf_op jit(solution)/shard_map/ppermute | solution.py:33

commit v3 on v1

--- a/solution.py
+++ b/solution.py
@@ -23,8 +23,8 @@
 
 def exchange(to_even, to_odd, axis):
     count = lax.axis_size(axis)
+    even_side = lax.ppermute(to_even, axis, pair_even(count))
     odd_side = lax.ppermute(to_odd, axis, pair_odd(count))
-    even_side = lax.ppermute(to_even, axis, pair_even(count))
     return even_side, odd_side
 
 

time: 21 us -> 21 us (level)
  no operation moved by 1% of the time
where the time goes in v3:
time: 21 us; the launch traced here: 20.8 us
  starting transfers between devices  10 us (48%)
  Pallas kernels  7.97 us (38%)
  waiting for transfers between devices  2.12 us (10%)
  between operations  0.71 us (3%)
    ppermute x5, starting transfers between devices, shift(): lax.ppermute(block, axis, [(i, (i + turn) % count) for i in range(count)])  6.88 us
    ppermute x1, starting transfers between devices, exchange(): odd_side = lax.ppermute(to_odd, axis, pair_odd(count))  2.61 us
    ppermute x5, waiting for transfers between devices, shift(): lax.ppermute(block, axis, [(i, (i + turn) % count) for i in range(count)])  2.12 us
    pallas_call x1, Pallas kernels, local(): pl.pallas_call(pack_kernel, out_shape=(pltpu.VMEM((levels, width), f32),...  1.68 us
    pallas_call x1, Pallas kernels, local(): pl.pallas_call(inner_kernel, out_shape=(pltpu.VMEM((rows, levels, width),...  1.67 us
    pallas_call x1, Pallas kernels, local(): pl.pallas_call(start_kernel, out_shape=tuple((pltpu.VMEM(value.shape, val...  1.54 us
    pallas_call x1, Pallas kernels, local(): pl.pallas_call(settle_kernel, out_shape=(shape_of((rows, levels, width)),...  1.02 us
    pallas_call x1, Pallas kernels, local(): pl.pallas_call(make_last_kernel(len(gathered)), out_shape=(shape_of(ocean...  1.02 us
  transfers between devices with their start and end apart: 7, of which 3 were waited for; matrix products, arithmetic and copies ran while one was open for 0% of the time, Pallas kernels for 21%

profile of v3, /device:TPU:0, one launch (start us, length us, event | category | flops | bytes accessed | tf_op | source)
XLA Modules:
  0.0 20.8 jit_solution(9341752709283928230)
XLA Ops:
  0.6 1.7 %pack.1 = (f32[64,128]{1,0:T(8,128)S(1)}, bf16[64,128]{1,0:T(8,128)(2,1)S(1)}, bf16[64,128]{1,0:T(8,128)(2,1)S(1)}, f32[24,64,128]{2,1,0:T(8,128)S(1)}, bf16[2,2...) custom-call(f32[24,64,128]{2,1,0:T(8,128)} %air.1, bf16[2,24,64,128]{3,2,1,0:T(8,128)(2,1)} %wind.1, ...), custom_call_target="tpu_custom_call" | custom-call | tf_op jit(solution)/shard_map/pack/pallas_call | solution.py:562
  2.3 0.5 %collective-permute-start = (bf16[64,128]{1,0:T(8,128)(2,1)S(1)}, bf16[64,128]{1,0:T(8,128)(2,1)S(1)}, u32[]{:S(2)}, u32[]{:S(2)}) collective-permute-start(bf16[64,128]{1,0:T(8,128)(2,1)S(1)} %get-tuple-element.40), channel_id=1, source_target_pairs={{0,1},{1,0},{2,3},{3,2},{4,5},{5,4},{6,7},{7,6},{8,9},{9,8},{10,11... | collective-permute-start | bytes 49160 | tf_op jit(solution)/shard_map/ppermute | solution.py:26
  2.8 2.6 %collective-permute-start.1 = (bf16[64,128]{1,0:T(8,128)(2,1)S(1)}, bf16[64,128]{1,0:T(8,128)(2,1)S(1)}, u32[]{:S(2)}, u32[]{:S(2)}) collective-permute-start(bf16[64,128]{1,0:T(8,128)(2,1)S(1)} %get-tuple-element.41), channel_id=1, source_target_pairs={{1,2},{3,0},{2,1},{0,3},{5,6},{7,4},{6,5},{4,7},{9,10},{11,8},{10,... | collective-permute-start | bytes 49160 | tf_op jit(solution)/shard_map/ppermute | solution.py:27
  5.5 1.5 %start.1 = (s32[24,128]{1,0:T(8,128)S(1)}, f32[24,128]{1,0:T(8,128)S(1)}, f32[16,32,128]{2,1,0:T(8,128)S(1)}, f32[80,768]{1,0:T(8,128)S(1)}, f32[24,128]{1,0:T(8...) custom-call(bf16[2,24,64,128]{3,2,1,0:T(8,128)(2,1)S(1)} %get-tuple-, ...), custom_call_target="tpu_custom_call" | custom-call | tf_op jit(solution)/shard_map/start/pallas_call | solution.py:595
  7.0 0.0 collective-permute-done.even_side
  7.0 0.0 collective-permute-done.1.odd_side
  7.0 0.1 edge.2
  7.1 1.6 %collective-permute-start.3 = (bf16[208,128]{1,0:T(8,128)(2,1)S(1)}, bf16[208,128]{1,0:T(8,128)(2,1)S(1)}, u32[]{:S(2)}, u32[]{:S(2)}) collective-permute-start(bf16[208,128]{1,0:T(8,128)(2,1)S(1)} %get-tuple-element.48), channel_id=1, source_target_pairs={{0,4},{4,8},{8,12},{12,16},{16,20},{20,24},{24,28},{28,0},{1,5},{5... | collective-permute-start | bytes 159752 | tf_op jit(solution)/shard_map/ppermute | solution.py:33
  8.8 0.1 edge.3
  8.9 3.2 %collective-permute-start.2 = (bf16[208,128]{1,0:T(8,128)(2,1)S(1)}, bf16[208,128]{1,0:T(8,128)(2,1)S(1)}, u32[]{:S(2)}, u32[]{:S(2)}) collective-permute-start(bf16[208,128]{1,0:T(8,128)(2,1)S(1)} %get-tuple-element.47), channel_id=1, source_target_pairs={{0,28},{4,0},{8,4},{12,8},{16,12},{20,16},{24,20},{28,24},{1,29},{... | collective-permute-start | bytes 159752 | tf_op jit(solution)/shard_map/ppermute | solution.py:33
  12.1 1.7 %inner.1 = (f32[24,64,128]{2,1,0:T(8,128)S(1)}, f32[4,64,128]{2,1,0:T(8,128)S(1)}, f32[24,128]{1,0:T(8,128)S(1)}) custom-call(f32[24,64,128]{2,1,0:T(8,128)S(1)} %get-tuple-element.38.air, bf16[2,24,64,128]{3,2,1,0:T(8,128)(2,1)S(1)} %get-tuple-element.39.winds.wind, bf16[64,192]{1,0:T(8,128)(2,1)S(1)} %get-tuple-element.50.stack_ref, ...), custom_call_target="tpu_custom_call" | custom-call | tf_op jit(solution)/shard_map/inner/pallas_call | solution.py:632
  13.7 0.5 %collective-permute-done.3.below_ref = bf16[208,128]{1,0:T(8,128)(2,1)S(1)} collective-permute-done((bf16[208,128]{1,0:T(8,128)(2,1)S(1)}, bf16[208,128]{1,0:T(8,128)(2,1)S(1)}, u32[]{:S(2)}, u32[]{:S(2)}) %collective-permute-start.3) | collective-permute-done | bytes 53280 | tf_op jit(solution)/shard_map/ppermute | solution.py:33
  14.2 0.0 collective-permute-done.2.above_ref
  14.2 0.8 %outer.1 = (f32[4,64,128]{2,1,0:T(8,128)S(1)}, f32[24,128]{1,0:T(8,128)S(1)}, f32[32,128]{1,0:T(8,128)S(1)}) custom-call(bf16[208,128]{1,0:T(8,128)(2,1)S(1)} %collective-permute-done.2.above_ref, bf16[208,128]{1,0:T(8,128)(2,1)S(1)} %collective-permute-done.3.below_ref, f32[2,64,128]{2,1,0:T(8,128)S(1)} %get-tuple-element.49.partial_low, ...), custom_call_target="tpu_custom_call" | custom-call | tf_op jit(solution)/shard_map/outer/pallas_call | solution.py:646
  15.1 0.9 %collective-permute-start.6 = (f32[32,128]{1,0:T(8,128)S(1)}, f32[32,128]{1,0:T(8,128)S(1)}, u32[]{:S(2)}, u32[]{:S(2)}) collective-permute-start(f32[32,128]{1,0:T(8,128)S(1)} %get-tuple-element.63.refs_0_), channel_id=1, source_target_pairs={{0,3},{1,0},{2,1},{3,2},{4,7},{5,4},{6,5},{7,6},{8,11},{9,8},{10,9... | collective-permute-start | bytes 49160 | tf_op jit(solution)/shard_map/ppermute | solution.py:33
  16.0 0.0 collective-permute-start.5
  16.0 1.1 %collective-permute-start.4 = (f32[32,128]{1,0:T(8,128)S(1)}, f32[32,128]{1,0:T(8,128)S(1)}, u32[]{:S(2)}, u32[]{:S(2)}) collective-permute-start(f32[32,128]{1,0:T(8,128)S(1)} %get-tuple-element.63.refs_0_), channel_id=1, source_target_pairs={{0,2},{1,3},{2,0},{3,1},{4,6},{5,7},{6,4},{7,5},{8,10},{9,11},{10,... | collective-permute-start | bytes 49160 | tf_op jit(solution)/shard_map/ppermute | solution.py:33
  17.1 1.0 %settle.1 = (f32[24,64,128]{2,1,0:T(8,128)}, f32[80,768]{1,0:T(8,128)S(1)}, f32[80,128]{1,0:T(8,128)S(1)}, f32[24,128]{1,0:T(8,128)S(1)}, bf16[1536,128]{1,0:T(8,128)(2,1)S(1)}) custom-call(f32[4,64,128]{2,1,0:T(8,128)S(1)} %get-tuple-element.58.edges, f32[24,64,128]{2,1,0:T(8,128)S(1)} %get-tuple-element.59.inner, ...), custom_call_target="tpu_custom_call" | custom-call | tf_op jit(solution)/shard_map/settle/pallas_call | solution.py:684
  18.2 0.0 collective-permute-done.6.refs_3_
  18.2 1.0 %collective-permute-done.5.refs_2_ = f32[32,128]{1,0:T(8,128)S(1)} collective-permute-done((f32[32,128]{1,0:T(8,128)S(1)}, f32[32,128]{1,0:T(8,128)S(1)}, u32[]{:S(2)}, u32[]{:S(2)}) %collective-permute-start.5) | collective-permute-done | bytes 16416 | tf_op jit(solution)/shard_map/ppermute | solution.py:33
  19.2 0.6 %collective-permute-done.4.refs_1_ = f32[32,128]{1,0:T(8,128)S(1)} collective-permute-done((f32[32,128]{1,0:T(8,128)S(1)}, f32[32,128]{1,0:T(8,128)S(1)}, u32[]{:S(2)}, u32[]{:S(2)}) %collective-permute-start.4) | collective-permute-done | bytes 16416 | tf_op jit(solution)/shard_map/ppermute | solution.py:33
  19.8 1.0 %last.1 = (f32[80,768]{1,0:T(8,128)}, f32[24,128]{1,0:T(8,128)}) custom-call(f32[32,128]{1,0:T(8,128)S(1)} %get-tuple-element.63.refs_0_, f32[32,128]{1,0:T(8,128)S(1)} %collective-permute-done.4.refs_1_, f32[32,128]{1,0:T(8,128)S(1)} %collective-permute-done.5.refs_2_, f32[32,128]{1,0:T(8,128)S(1)} %collective-permute-done.6.refs_3_, ...), custom_call_target="tpu_custom_call" | custom-call | tf_op jit(solution)/shard_map/last/pallas_call | solution.py:700
Async XLA Ops:
  2.3 4.7 %collective-permute-start = (bf16[64,128]{1,0:T(8,128)(2,1)S(1)}, bf16[64,128]{1,0:T(8,128)(2,1)S(1)}, u32[]{:S(2)}, u32[]{:S(2)}) collective-permute-start(bf16[64,128]{1,0:T(8,128)(2,1)S(1)} %get-tuple-element.40), channel_id=1, source_target_pairs={{0,1},{1,0},{2,3},{3,2},{4,5},{5,4},{6,7},{7,6},{8,9},{9,8},{10,11... | collective-permute-start | bytes 49160 | tf_op jit(solution)/shard_map/ppermute | solution.py:26
  2.8 4.2 %collective-permute-start.1 = (bf16[64,128]{1,0:T(8,128)(2,1)S(1)}, bf16[64,128]{1,0:T(8,128)(2,1)S(1)}, u32[]{:S(2)}, u32[]{:S(2)}) collective-permute-start(bf16[64,128]{1,0:T(8,128)(2,1)S(1)} %get-tuple-element.41), channel_id=1, source_target_pairs={{1,2},{3,0},{2,1},{0,3},{5,6},{7,4},{6,5},{4,7},{9,10},{11,8},{10,... | collective-permute-start | bytes 49160 | tf_op jit(solution)/shard_map/ppermute | solution.py:27
  7.1 7.1 %collective-permute-start.3 = (bf16[208,128]{1,0:T(8,128)(2,1)S(1)}, bf16[208,128]{1,0:T(8,128)(2,1)S(1)}, u32[]{:S(2)}, u32[]{:S(2)}) collective-permute-start(bf16[208,128]{1,0:T(8,128)(2,1)S(1)} %get-tuple-element.48), channel_id=1, source_target_pairs={{0,4},{4,8},{8,12},{12,16},{16,20},{20,24},{24,28},{28,0},{1,5},{5... | collective-permute-start | bytes 159752 | tf_op jit(solution)/shard_map/ppermute | solution.py:33
  8.9 5.4 %collective-permute-start.2 = (bf16[208,128]{1,0:T(8,128)(2,1)S(1)}, bf16[208,128]{1,0:T(8,128)(2,1)S(1)}, u32[]{:S(2)}, u32[]{:S(2)}) collective-permute-start(bf16[208,128]{1,0:T(8,128)(2,1)S(1)} %get-tuple-element.47), channel_id=1, source_target_pairs={{0,28},{4,0},{8,4},{12,8},{16,12},{20,16},{24,20},{28,24},{1,29},{... | collective-permute-start | bytes 159752 | tf_op jit(solution)/shard_map/ppermute | solution.py:33
  15.1 3.1 %collective-permute-start.6 = (f32[32,128]{1,0:T(8,128)S(1)}, f32[32,128]{1,0:T(8,128)S(1)}, u32[]{:S(2)}, u32[]{:S(2)}) collective-permute-start(f32[32,128]{1,0:T(8,128)S(1)} %get-tuple-element.63.refs_0_), channel_id=1, source_target_pairs={{0,3},{1,0},{2,1},{3,2},{4,7},{5,4},{6,5},{7,6},{8,11},{9,8},{10,9... | collective-permute-start | bytes 49160 | tf_op jit(solution)/shard_map/ppermute | solution.py:33
  16.0 3.2 %collective-permute-start.5 = (f32[32,128]{1,0:T(8,128)S(1)}, f32[32,128]{1,0:T(8,128)S(1)}, u32[]{:S(2)}, u32[]{:S(2)}) collective-permute-start(f32[32,128]{1,0:T(8,128)S(1)} %get-tuple-element.63.refs_0_), channel_id=1, source_target_pairs={{0,1},{1,2},{2,3},{3,0},{4,5},{5,6},{6,7},{7,4},{8,9},{9,10},{10,1... | collective-permute-start | bytes 49160 | tf_op jit(solution)/shard_map/ppermute | solution.py:33
  16.0 3.8 %collective-permute-start.4 = (f32[32,128]{1,0:T(8,128)S(1)}, f32[32,128]{1,0:T(8,128)S(1)}, u32[]{:S(2)}, u32[]{:S(2)}) collective-permute-start(f32[32,128]{1,0:T(8,128)S(1)} %get-tuple-element.63.refs_0_), channel_id=1, source_target_pairs={{0,2},{1,3},{2,0},{3,1},{4,6},{5,7},{6,4},{7,5},{8,10},{9,11},{10,... | collective-permute-start | bytes 49160 | tf_op jit(solution)/shard_map/ppermute | solution.py:33
